TPU v7x, 32 devices: a whole 2x2x4 slice. The times are simulated.
32 devices in a mesh: ctx: 8 (over y, x, core), head: 4 (over z).
Axes of the slice: x: 2, y: 2, z: 4, core: 2. Of those that a mesh axis runs over, the one named last changes fastest.
Arguments:
- lin_q: bfloat16 [2048, 8192], P('ctx', 'head'), may hold values from -4 to 4
- lin_k: bfloat16 [2048, 8192], P('ctx', 'head'), may hold values from -4 to 4
- lin_v: bfloat16 [2048, 8192], P('ctx', 'head'), may hold values from -6 to 6
- log_decay: float32 [64, 2048], P('head', 'ctx'), may hold values from -1 to 0
- lin_gain: float32 [8192], P('head'), may hold values from 0.1 to 1.9
- soft_q: bfloat16 [2048, 8192], P(('ctx', 'head')), may hold values from -200 to 200
- soft_kv: bfloat16 [2048, 2048], P(('ctx', 'head')), may hold values from -8 to 8
Outputs:
- lin_out: bfloat16 [2048, 8192], P('ctx', 'head')
- soft_out: bfloat16 [2048, 8192], P(('ctx', 'head'))
All inputs are finite; a program needn't handle non-finite values.
Results may differ from a plain program's by a relative error of at most 0.013.
Values may be sent and summed in bfloat16 or wider, within the bound.
A program may use at most 64 MiB of HBM per device.

v0:
```python
import math

import jax
import jax.numpy as jnp
from jax import lax
from jax.sharding import PartitionSpec as P


def block_local(kb, gb):
    cum = jnp.cumsum(gb, axis=1)
    keys_scaled = (kb.astype(jnp.float32) * jnp.exp(cum[:, -1:] - cum).T[:, :, None]).astype(
        jnp.bfloat16
    )
    return (cum, keys_scaled)


def block_output(qb, kb, vb, cum, state):
    size = cum.shape[1]
    pos = jnp.arange(size)
    causal = pos[:, None] >= pos[None, :]
    diff = cum[:, :, None] - cum[:, None, :]
    weight = jnp.where(causal[None], jnp.exp(jnp.minimum(diff, 0.0)), 0.0)
    scores = jnp.einsum("thd,shd->hts", qb, kb, preferred_element_type=jnp.float32)
    probs = (scores * weight).astype(jnp.bfloat16)
    intra = jnp.einsum("hts,shd->thd", probs, vb, preferred_element_type=jnp.float32)
    inter = jnp.einsum(
        "thd,hde->the", qb, state.astype(jnp.bfloat16), preferred_element_type=jnp.float32
    )
    return intra + jnp.exp(cum).T[:, :, None] * inter


def join_states(earlier, later):
    return (later[0], jnp.exp(later[0])[:, None, None] * earlier[1] + later[1])


def lightning_part(lin_q, lin_k, lin_v, log_decay, lin_gain):
    tok, width = lin_q.shape
    heads = log_decay.shape[0]
    dim = width // heads
    q = lin_q.reshape(tok, heads, dim)
    k = lin_k.reshape(tok, heads, dim)
    v = lin_v.reshape(tok, heads, dim)
    total = (jnp.zeros((heads,), jnp.float32), jnp.zeros((heads, dim, dim), jnp.float32))
    cum, keys_scaled = block_local(k, log_decay)
    local = jnp.einsum("shd,she->hde", keys_scaled, v, preferred_element_type=jnp.float32)
    total = join_states(total, (cum[:, -1], local))
    logs = lax.all_gather(total[0][None], "ctx", axis=0, tiled=True)
    mine = lax.axis_index("ctx")
    csum = jnp.cumsum(logs, axis=0)
    before = jnp.sum(jnp.where((jnp.arange(logs.shape[0]) < mine)[:, None], logs, 0.0), axis=0)
    piece = lax.all_gather(total[1][None].astype(jnp.bfloat16), "ctx", axis=0, tiled=True).astype(
        jnp.float32
    )
    rows = piece.shape[0]
    idx = jnp.arange(rows)
    live = (idx < mine)[:, None]
    decay_factor = jnp.exp(jnp.where(live, before[None] - csum, -jnp.inf))
    state = jnp.zeros((heads, dim, dim), jnp.float32) + jnp.einsum(
        "jh,jhde->hde", decay_factor, piece, precision=lax.Precision.HIGHEST
    )
    mixed = block_output(q, k, v, cum, state)
    rms = jnp.sqrt(jnp.mean(mixed * mixed, axis=-1, keepdims=True) + 1e-05)
    outputs = mixed / rms * lin_gain.reshape(heads, dim)
    return outputs.reshape(tok, width).astype(jnp.bfloat16)


def softmax_part(soft_q, soft_kv, dim):
    local_q, local_kv = (
        lax.all_to_all(soft_q, "head", split_axis=1, concat_axis=0, tiled=True),
        lax.all_to_all(soft_kv, "head", split_axis=1, concat_axis=0, tiled=True),
    )
    tok = local_q.shape[0]
    half = tok // 2
    kvl = local_kv.shape[1] // (2 * dim)
    group = local_q.shape[1] // (dim * kvl)
    mine = lax.axis_index("ctx")
    first_q = local_q[:half]
    second_q = local_q[half:]
    second_start = mine * tok + half
    first_start = mine * tok
    first_pos = first_start + jnp.arange(half)
    second_pos = second_start + jnp.arange(half)
    first_heads = first_q.reshape(half, kvl, group, dim)
    second_heads = second_q.reshape(half, kvl, group, dim)
    scale = dim ** (-0.5)

    def update(carry, queries, qpos, kblock, kstart):
        peak, total, acc = carry
        size = kblock.shape[0]
        pair = kblock.reshape(size, kvl, 2, dim)
        key_matrix = pair[:, :, 0]
        value_rows = pair[:, :, 1]
        kpos = kstart + jnp.arange(size)
        mask = (kpos[None, :] <= qpos[:, None])[None, None]
        scores = (
            jnp.einsum("qngd,knd->ngqk", queries, key_matrix, preferred_element_type=jnp.float32)
            * scale
        )
        scores = jnp.where(mask, scores, -1e30)
        newpeak = jnp.maximum(peak, jnp.max(scores, axis=-1))
        weights = jnp.where(mask, jnp.exp(scores - newpeak[..., None]), 0.0)
        decay_factor = jnp.exp(peak - newpeak)
        total = total * decay_factor + jnp.sum(weights, axis=-1)
        acc = acc * decay_factor[..., None] + jnp.einsum(
            "ngqk,knd->ngqd",
            weights.astype(jnp.bfloat16),
            value_rows,
            preferred_element_type=jnp.float32,
        )
        return (newpeak, total, acc)

    def guarded(carry, queries, qpos, kblock, kstart):
        return update(carry, queries, qpos, kblock, kstart)

    def start_carry():
        return (
            jnp.full((kvl, group, half), -1e30, jnp.float32),
            jnp.zeros((kvl, group, half), jnp.float32),
            jnp.zeros((kvl, group, half, dim), jnp.float32),
        )

    def finish(carry):
        peak, total, acc = carry
        result = acc / total[..., None]
        return result.transpose(2, 0, 1, 3).reshape(half, kvl * group * dim).astype(jnp.bfloat16)

    piece = lax.all_gather(local_kv, "ctx", axis=0, tiled=True)
    rows = piece.shape[0]
    width = math.gcd(rows, 512)

    def step(index, inner):
        kblock = lax.dynamic_slice_in_dim(piece, index * width, width, 0)
        kstart = index * width
        early = guarded(inner[0], first_heads, first_pos, kblock, kstart)
        later = guarded(inner[1], second_heads, second_pos, kblock, kstart)
        return (early, later)

    early, later = lax.fori_loop(0, rows // width, step, (start_carry(), start_carry()))
    first_out = finish(early)
    second_out = finish(later)
    result = jnp.concatenate([first_out, second_out], axis=0)
    return lax.all_to_all(result, "head", split_axis=0, concat_axis=1, tiled=True)


def body(lin_q, lin_k, lin_v, log_decay, lin_gain, soft_q, soft_kv):
    heads = log_decay.shape[0]
    dim = lin_q.shape[1] // heads
    lin_out = lightning_part(lin_q, lin_k, lin_v, log_decay, lin_gain)
    soft_out = softmax_part(soft_q, soft_kv, dim)
    return (lin_out, soft_out)


def solution(mesh):
    return jax.shard_map(
        body,
        mesh=mesh,
        in_specs=(
            P("ctx", "head"),
            P("ctx", "head"),
            P("ctx", "head"),
            P("head", "ctx"),
            P("head"),
            P(("ctx", "head"), None),
            P(("ctx", "head"), None),
        ),
        out_specs=(P("ctx", "head"), P(("ctx", "head"), None)),
        check_vma=False,
    )
```

profile of v0, /device:TPU:0, one launch (start us, length us, event | category | flops | bytes accessed | tf_op | source)
XLA Modules:
  0.0 144.2 jit_solution(18181334939448320045)
XLA Ops:
  7.2 1.1 copy.158
  8.4 15.1 %all_to_all.54 = bf16[64,4,512]{2,0,1:T(8,128)(2,1)} all-to-all(bf16[64,4,512]{2,0,1:T(8,128)(2,1)S(1)} %bitcast.190), channel_id=1, replica_groups=mesh['ctx'=8,'head'=4] {'head'}, dimensions={1} | all-to-all | bytes 524288 | tf_op jit(solution)/shard_map/all_to_all | solution.py:70
  23.5 2.3 %copy.157 = bf16[8,4,8,2048]{3,2,0,1:T(8,128)(2,1)} copy(bf16[8,4,8,2048]{3,2,1,0:T(8,128)(2,1)} %bitcast.185) | data formatting | bytes 2097152 | tf_op jit(solution)/shard_map/all_to_all | solution.py:69
  25.8 3.5 %all-to-all-start.1 = ((bf16[64,4,2048]{2,0,1:T(8,128)(2,1)}), bf16[64,4,2048]{2,0,1:T(8,128)(2,1)S(1)}, u32[]{:S(2)}, u32[]{:S(2)}) async-start(bf16[64,4,2048]{2,0,1:T(8,128)(2,1)} %bitcast.143), calls=%async_computation.1 | async-start | bytes 2097152 | tf_op jit(solution)/shard_map/all_to_all | solution.py:69
  29.4 0.6 reduce-window.6
  30.0 0.2 slice_reduce_fusion
  30.2 1.3 copy.120
  31.6 0.2 slice_reduce_fusion.1
  31.8 2.8 %fusion.34 = bf16[16,128,128]{2,1,0:T(8,128)(2,1)} fusion(bf16[256,16,128]{0,2,1:T(8,128)(2,1)} %bitcast.186, f32[256,16]{0,1:T(8,128)S(1)} %get-tuple-element.349, f32[16]{0:T(128)S(1)} %exponential_multiply_fusion, bf16[256,2048]{1,0:T(8,128)(2,1)} %param.11), kind=kOutput, calls=%fused_computation.53 | convolution fusion | flops 136314880 | bytes 2637888 | tf_op jit(solution)/shard_map/shd,she->hde/dot_general | solution.py:45
  34.8 19.0 %all-to-all-done.1 = bf16[64,4,2048]{2,0,1:T(8,128)(2,1)S(1)} async-done(((bf16[64,4,2048]{2,0,1:T(8,128)(2,1)}), bf16[64,4,2048]{2,0,1:T(8,128)(2,1)S(1)}, u32[]{:S(2)}, u32[]{:S(2)}) %all-to-all-start.1) | async-done | bytes 1048608 | tf_op jit(solution)/shard_map/all_to_all | solution.py:69
  54.4 38.8 %while.24 = (s32[]{:T(128)}, f32[2,8,128]{2,1,0:T(8,128)S(1)}, f32[2,8,128]{2,1,0:T(8,128)S(1)}, f32[2,8,128,128]{3,2,1,0:T(8,128)}, f32[2,8,128]{2,1,0:T(8,128)...) while((s32[]{:T(128)}, f32[2,8,128]{2,1,0:T(8,128)S(1)}, ...), condition=%wide.region_10.11_spmd.clone, body=%wide.region_5.10_spmd.clone.sunk | while | flops 1102729984 | bytes 51124564 | solution.py:138
  54.5 0.1 broadcast_compare_fusion.3
  54.6 1.1 constant_dynamic-slice_fusion.2
  55.7 0.2 copy.160
  55.9 0.8 fusion.74
  56.8 1.0 fusion.75
  57.8 0.8 fusion.73
  58.7 1.0 fusion.76
  59.7 1.7 %fusion.79 = f32[2,8,128,128]{3,2,1,0:T(8,128)S(1)} fusion(f32[2,512,128,8]{2,1,3,0:T(8,128)S(1)} %get-tuple-element.441, f32[2,8,128]{2,1,0:T(8,128)S(1)} %select_maximum_fusion.5, pred[128,512]{0,1:T(8,128)(4,1)S(1)} %get-tuple-element.440, f32[2,8,128,128]{3,2,1,0:T(8,128)S(1)} %copy-done.4, f32[2,8,128]{2,1,0:T(8,128)S(1)} %get-tuple-element.447, ...), kind=kOutput, calls=%fused_computation.17.clone.1 | convolution fusion | flops 274464768 | bytes 6635521 | tf_op jit(solution)/shard_map/while/body/eval_jaxpr/ngqk,knd->ngqd/dot_general | solution.py:104
  61.5 1.7 %fusion.78 = f32[2,8,128,128]{3,2,1,0:T(8,128)S(1)} fusion(f32[2,512,128,8]{2,1,3,0:T(8,128)S(1)} %get-tuple-element.443, f32[2,8,128]{2,1,0:T(8,128)S(1)} %select_maximum_fusion.4, pred[128,512]{0,1:T(8,128)(4,1)S(1)} %get-tuple-element.438, f32[2,8,128,128]{3,2,1,0:T(8,128)S(1)} %copy-done.6, f32[2,8,128]{2,1,0:T(8,128)S(1)} %get-tuple-element.445, ...), kind=kOutput, calls=%fused_computation.16.clone.1 | convolution fusion | flops 274464768 | bytes 6635521 | tf_op jit(solution)/shard_map/while/body/eval_jaxpr/ngqk,knd->ngqd/dot_general | solution.py:104
  63.2 0.9 copy-done.7
  64.3 1.1 constant_dynamic-slice_fusion.2
  65.4 0.2 copy.160
  65.6 0.8 fusion.74
  66.5 1.0 fusion.75
  67.5 0.8 fusion.73
  68.3 1.0 fusion.76
  69.4 1.7 %fusion.79 = f32[2,8,128,128]{3,2,1,0:T(8,128)S(1)} fusion(f32[2,512,128,8]{2,1,3,0:T(8,128)S(1)} %get-tuple-element.441, f32[2,8,128]{2,1,0:T(8,128)S(1)} %select_maximum_fusion.5, pred[128,512]{0,1:T(8,128)(4,1)S(1)} %get-tuple-element.440, f32[2,8,128,128]{3,2,1,0:T(8,128)S(1)} %copy-done.4, f32[2,8,128]{2,1,0:T(8,128)S(1)} %get-tuple-element.447, ...), kind=kOutput, calls=%fused_computation.17.clone.1 | convolution fusion | flops 274464768 | bytes 6635521 | tf_op jit(solution)/shard_map/while/body/eval_jaxpr/ngqk,knd->ngqd/dot_general | solution.py:104
  71.1 1.7 %fusion.78 = f32[2,8,128,128]{3,2,1,0:T(8,128)S(1)} fusion(f32[2,512,128,8]{2,1,3,0:T(8,128)S(1)} %get-tuple-element.443, f32[2,8,128]{2,1,0:T(8,128)S(1)} %select_maximum_fusion.4, pred[128,512]{0,1:T(8,128)(4,1)S(1)} %get-tuple-element.438, f32[2,8,128,128]{3,2,1,0:T(8,128)S(1)} %copy-done.6, f32[2,8,128]{2,1,0:T(8,128)S(1)} %get-tuple-element.445, ...), kind=kOutput, calls=%fused_computation.16.clone.1 | convolution fusion | flops 274464768 | bytes 6635521 | tf_op jit(solution)/shard_map/while/body/eval_jaxpr/ngqk,knd->ngqd/dot_general | solution.py:104
  72.9 0.9 copy-done.7
  74.0 1.2 constant_dynamic-slice_fusion.2
  75.2 0.2 copy.160
  75.4 0.8 fusion.74
  76.3 1.0 fusion.75
  77.3 0.8 fusion.73
  78.1 1.0 fusion.76
  79.2 1.7 %fusion.79 = f32[2,8,128,128]{3,2,1,0:T(8,128)S(1)} fusion(f32[2,512,128,8]{2,1,3,0:T(8,128)S(1)} %get-tuple-element.441, f32[2,8,128]{2,1,0:T(8,128)S(1)} %select_maximum_fusion.5, pred[128,512]{0,1:T(8,128)(4,1)S(1)} %get-tuple-element.440, f32[2,8,128,128]{3,2,1,0:T(8,128)S(1)} %copy-done.4, f32[2,8,128]{2,1,0:T(8,128)S(1)} %get-tuple-element.447, ...), kind=kOutput, calls=%fused_computation.17.clone.1 | convolution fusion | flops 274464768 | bytes 6635521 | tf_op jit(solution)/shard_map/while/body/eval_jaxpr/ngqk,knd->ngqd/dot_general | solution.py:104
  80.9 1.7 %fusion.78 = f32[2,8,128,128]{3,2,1,0:T(8,128)S(1)} fusion(f32[2,512,128,8]{2,1,3,0:T(8,128)S(1)} %get-tuple-element.443, f32[2,8,128]{2,1,0:T(8,128)S(1)} %select_maximum_fusion.4, pred[128,512]{0,1:T(8,128)(4,1)S(1)} %get-tuple-element.438, f32[2,8,128,128]{3,2,1,0:T(8,128)S(1)} %copy-done.6, f32[2,8,128]{2,1,0:T(8,128)S(1)} %get-tuple-element.445, ...), kind=kOutput, calls=%fused_computation.16.clone.1 | convolution fusion | flops 274464768 | bytes 6635521 | tf_op jit(solution)/shard_map/while/body/eval_jaxpr/ngqk,knd->ngqd/dot_general | solution.py:104
  82.7 0.9 copy-done.7
  83.8 1.1 constant_dynamic-slice_fusion.2
  84.9 0.2 copy.160
  85.1 0.8 fusion.74
  85.9 1.0 fusion.75
  87.0 0.8 fusion.73
  87.8 1.0 fusion.76
  88.9 1.7 %fusion.79 = f32[2,8,128,128]{3,2,1,0:T(8,128)S(1)} fusion(f32[2,512,128,8]{2,1,3,0:T(8,128)S(1)} %get-tuple-element.441, f32[2,8,128]{2,1,0:T(8,128)S(1)} %select_maximum_fusion.5, pred[128,512]{0,1:T(8,128)(4,1)S(1)} %get-tuple-element.440, f32[2,8,128,128]{3,2,1,0:T(8,128)S(1)} %copy-done.4, f32[2,8,128]{2,1,0:T(8,128)S(1)} %get-tuple-element.447, ...), kind=kOutput, calls=%fused_computation.17.clone.1 | convolution fusion | flops 274464768 | bytes 6635521 | tf_op jit(solution)/shard_map/while/body/eval_jaxpr/ngqk,knd->ngqd/dot_general | solution.py:104
  90.6 1.7 %fusion.78 = f32[2,8,128,128]{3,2,1,0:T(8,128)S(1)} fusion(f32[2,512,128,8]{2,1,3,0:T(8,128)S(1)} %get-tuple-element.443, f32[2,8,128]{2,1,0:T(8,128)S(1)} %select_maximum_fusion.4, pred[128,512]{0,1:T(8,128)(4,1)S(1)} %get-tuple-element.438, f32[2,8,128,128]{3,2,1,0:T(8,128)S(1)} %copy-done.6, f32[2,8,128]{2,1,0:T(8,128)S(1)} %get-tuple-element.445, ...), kind=kOutput, calls=%fused_computation.16.clone.1 | convolution fusion | flops 274464768 | bytes 6635521 | tf_op jit(solution)/shard_map/while/body/eval_jaxpr/ngqk,knd->ngqd/dot_general | solution.py:104
  92.3 0.9 copy-done.7
  93.3 1.6 %copy.101 = f32[2,8,128,128]{2,3,1,0:T(8,128)S(1)} copy(f32[2,8,128,128]{3,2,1,0:T(8,128)} %get-tuple-element.206) | data formatting | bytes 2097152 | tf_op jit(solution)/shard_map/while | solution.py:138
  94.8 1.6 %copy.100 = f32[2,8,128,128]{2,3,1,0:T(8,128)S(1)} copy(f32[2,8,128,128]{3,2,1,0:T(8,128)} %get-tuple-element.204) | data formatting | bytes 2097152 | tf_op jit(solution)/shard_map/while | solution.py:138
  96.4 0.3 divide_convert_fusion
  96.8 1.4 copy.102
  98.2 3.5 %all-to-all-start.2 = ((bf16[4,64,2048]{2,1,0:T(8,128)(2,1)}), bf16[4,64,2048]{2,1,0:T(8,128)(2,1)S(1)}, u32[]{:S(2)}, u32[]{:S(2)}) async-start(bf16[4,64,2048]{2,1,0:T(8,128)(2,1)} %bitcast.18), calls=%async_computation.2 | async-start | bytes 2097152 | tf_op jit(solution)/shard_map/all_to_all | solution.py:142
  101.8 0.6 dynamic-slice
  103.0 0.2 dynamic-update-slice
  103.3 13.2 %all-reduce = f32[128]{0:T(128)S(1)} all-reduce(f32[128]{0:T(128)S(1)} %dynamic-update-slice), channel_id=2, replica_groups=mesh['ctx'=8,'head'=4] {'ctx'}, use_global_device_ids=true, to_apply=%add | all-reduce | flops 128 | bytes 1024
  116.8 4.3 %fusion.33 = f32[16,256,128]{1,2,0:T(8,128)} fusion(bf16[256,16,128]{0,2,1:T(8,128)(2,1)S(1)} %bitcast.187, f32[16,256]{1,0:T(8,128)S(1)} %copy_bitcast_fusion.2, pred[256,256]{1,0:T(8,128)(4,1)S(1)} %iota_compare_fusion, bf16[256,2048]{1,0:T(8,128)(2,1)} %param.11, bf16[256,2048]{1,0:T(8,128)(2,1)S(1)} %copy-done), kind=kOutput, calls=%fused_computation.51 | convolution fusion | flops 542113792 | bytes 5324800 | tf_op jit(solution)/shard_map/hts,shd->thd/dot_general | solution.py:25
  121.1 5.7 %all-to-all-done.2 = bf16[4,64,2048]{2,1,0:T(8,128)(2,1)S(1)} async-done(((bf16[4,64,2048]{2,1,0:T(8,128)(2,1)}), bf16[4,64,2048]{2,1,0:T(8,128)(2,1)S(1)}, u32[]{:S(2)}, u32[]{:S(2)}) %all-to-all-start.2) | async-done | bytes 1048608 | tf_op jit(solution)/shard_map/all_to_all | solution.py:142
  126.8 1.0 copy.127
  127.9 4.1 %multiply_reduce_fusion = bf16[16,128,128]{2,1,0:T(8,128)(2,1)} fusion(bf16[16,8,128,128]{3,2,0,1:T(8,128)(2,1)} %bitcast.176, f32[16,8]{0,1:T(8,128)S(1)} %exponential_bitcast_fusion.2), kind=kLoop, calls=%fused_computation.44 | loop fusion | flops 6029312 | bytes 4719104
  132.0 2.0 %copy.115 = bf16[16,128,128]{1,2,0:T(8,128)(2,1)} copy(bf16[16,128,128]{2,1,0:T(8,128)(2,1)} %multiply_reduce_fusion) | data formatting | bytes 1048576 | tf_op jit(solution)/shard_map/jh,jhde->hde/dot_general | solution.py:58
  134.0 1.6 %multiply_reduce_fusion.1 = (f32[256,16]{0,1:T(8,128)S(1)}, f32[256,16,128]{0,2,1:T(8,128)S(1)}) fusion(bf16[16,128,128]{1,2,0:T(8,128)(2,1)} %copy.115, f32[256,16]{0,1:T(8,128)S(1)} %get-tuple-element.350, f32[16,256,128]{1,2,0:T(8,128)S(1)} %copy-done.1, bf16[256,2048]{1,0:T(8,128)(2,1)S(1)} %copy-done), kind=kOutput, calls=%fused_computation.49 | convolution fusion | flops 136310784 | bytes 5799936 | tf_op jit(solution)/shard_map/thd,hde->the/dot_general | solution.py:26
  135.6 0.3 multiply_convert_fusion.1
  136.0 1.4 copy.104
  (109 shorter events, 2.1 us)
Async XLA Ops:
  7.2 109.6 %copy-start = (bf16[256,2048]{1,0:T(8,128)(2,1)S(1)}, bf16[256,2048]{1,0:T(8,128)(2,1)}, u32[]{:S(2)}) copy-start(bf16[256,2048]{1,0:T(8,128)(2,1)} %param.9) | copy-start | bytes 3145732
  7.2 22.2 %copy-start.8 = (f32[16,256]{1,0:T(8,128)S(1)}, f32[16,256]{1,0:T(8,128)}, u32[]{:S(2)}) copy-start(f32[16,256]{1,0:T(8,128)} %param.12) | copy-start | bytes 49156
  7.2 23.0 %copy-start.2 = (bf16[256,2048]{1,0:T(8,128)(2,1)S(1)}, bf16[256,2048]{1,0:T(8,128)(2,1)}, u32[]{:S(2)}) copy-start(bf16[256,2048]{1,0:T(8,128)(2,1)} %param.10) | copy-start | bytes 3145732
  7.2 47.2 %all-gather.5.cloned.1.call-start = ((), (), s32[]{:S(2)}) async-start(), calls=%async_computation.3 | async-start | bytes 2359296 | tf_op jit(solution)/shard_map/all_gather | solution.py:127
  25.8 28.0 %all-to-all-start.1 = ((bf16[64,4,2048]{2,0,1:T(8,128)(2,1)}), bf16[64,4,2048]{2,0,1:T(8,128)(2,1)S(1)}, u32[]{:S(2)}, u32[]{:S(2)}) async-start(bf16[64,4,2048]{2,0,1:T(8,128)(2,1)} %bitcast.143), calls=%async_computation.1 | async-start | bytes 2097152 | tf_op jit(solution)/shard_map/all_to_all | solution.py:69
  29.3 98.5 %all-gather.7.cloned.1.call-start = ((), (), s32[]{:S(2)}) async-start(), calls=%async_computation.4 | async-start | bytes 4718592 | tf_op jit(solution)/shard_map/all_gather | solution.py:51
  57.8 1.9 %copy-start.4 = (f32[2,8,128,128]{3,2,1,0:T(8,128)S(1)}, f32[2,8,128,128]{3,2,1,0:T(8,128)}, u32[]{:S(2)}) copy-start(f32[2,8,128,128]{3,2,1,0:T(8,128)} %get-tuple-element.470) | copy-start | bytes 3145732 | tf_op jit(solution)/shard_map/while
  59.7 1.7 %copy-start.6 = (f32[2,8,128,128]{3,2,1,0:T(8,128)S(1)}, f32[2,8,128,128]{3,2,1,0:T(8,128)}, u32[]{:S(2)}) copy-start(f32[2,8,128,128]{3,2,1,0:T(8,128)} %get-tuple-element.467) | copy-start | bytes 3145732 | tf_op jit(solution)/shard_map/while
  61.4 1.7 %copy-start.5 = (f32[2,8,128,128]{3,2,1,0:T(8,128)}, f32[2,8,128,128]{3,2,1,0:T(8,128)S(1)}, u32[]{:S(2)}) copy-start(f32[2,8,128,128]{3,2,1,0:T(8,128)S(1)} %fusion.79) | copy-start | bytes 3145732 | tf_op jit(solution)/shard_map/while
  63.2 1.0 copy-start.7
  67.5 1.9 %copy-start.4 = (f32[2,8,128,128]{3,2,1,0:T(8,128)S(1)}, f32[2,8,128,128]{3,2,1,0:T(8,128)}, u32[]{:S(2)}) copy-start(f32[2,8,128,128]{3,2,1,0:T(8,128)} %get-tuple-element.470) | copy-start | bytes 3145732 | tf_op jit(solution)/shard_map/while
  69.4 1.7 %copy-start.6 = (f32[2,8,128,128]{3,2,1,0:T(8,128)S(1)}, f32[2,8,128,128]{3,2,1,0:T(8,128)}, u32[]{:S(2)}) copy-start(f32[2,8,128,128]{3,2,1,0:T(8,128)} %get-tuple-element.467) | copy-start | bytes 3145732 | tf_op jit(solution)/shard_map/while
  71.1 1.7 %copy-start.5 = (f32[2,8,128,128]{3,2,1,0:T(8,128)}, f32[2,8,128,128]{3,2,1,0:T(8,128)S(1)}, u32[]{:S(2)}) copy-start(f32[2,8,128,128]{3,2,1,0:T(8,128)S(1)} %fusion.79) | copy-start | bytes 3145732 | tf_op jit(solution)/shard_map/while
  72.8 1.0 copy-start.7
  77.3 1.9 %copy-start.4 = (f32[2,8,128,128]{3,2,1,0:T(8,128)S(1)}, f32[2,8,128,128]{3,2,1,0:T(8,128)}, u32[]{:S(2)}) copy-start(f32[2,8,128,128]{3,2,1,0:T(8,128)} %get-tuple-element.470) | copy-start | bytes 3145732 | tf_op jit(solution)/shard_map/while
  79.2 1.7 %copy-start.6 = (f32[2,8,128,128]{3,2,1,0:T(8,128)S(1)}, f32[2,8,128,128]{3,2,1,0:T(8,128)}, u32[]{:S(2)}) copy-start(f32[2,8,128,128]{3,2,1,0:T(8,128)} %get-tuple-element.467) | copy-start | bytes 3145732 | tf_op jit(solution)/shard_map/while
  80.9 1.7 %copy-start.5 = (f32[2,8,128,128]{3,2,1,0:T(8,128)}, f32[2,8,128,128]{3,2,1,0:T(8,128)S(1)}, u32[]{:S(2)}) copy-start(f32[2,8,128,128]{3,2,1,0:T(8,128)S(1)} %fusion.79) | copy-start | bytes 3145732 | tf_op jit(solution)/shard_map/while
  82.6 1.0 copy-start.7
  87.0 1.9 %copy-start.4 = (f32[2,8,128,128]{3,2,1,0:T(8,128)S(1)}, f32[2,8,128,128]{3,2,1,0:T(8,128)}, u32[]{:S(2)}) copy-start(f32[2,8,128,128]{3,2,1,0:T(8,128)} %get-tuple-element.470) | copy-start | bytes 3145732 | tf_op jit(solution)/shard_map/while
  88.9 1.7 %copy-start.6 = (f32[2,8,128,128]{3,2,1,0:T(8,128)S(1)}, f32[2,8,128,128]{3,2,1,0:T(8,128)}, u32[]{:S(2)}) copy-start(f32[2,8,128,128]{3,2,1,0:T(8,128)} %get-tuple-element.467) | copy-start | bytes 3145732 | tf_op jit(solution)/shard_map/while
  90.6 1.7 %copy-start.5 = (f32[2,8,128,128]{3,2,1,0:T(8,128)}, f32[2,8,128,128]{3,2,1,0:T(8,128)S(1)}, u32[]{:S(2)}) copy-start(f32[2,8,128,128]{3,2,1,0:T(8,128)S(1)} %fusion.79) | copy-start | bytes 3145732 | tf_op jit(solution)/shard_map/while
  92.3 1.0 copy-start.7
  96.4 5.4 %copy-start.10 = (u32[32]{0:T(128)S(1)}, u32[32]{0:T(128)}, u32[]{:S(2)}) copy-start(u32[32]{0:T(128)} %constant.87) | copy-start | bytes 388
  96.7 20.1 %copy-start.3 = (bf16[256,2048]{0,1:T(8,128)(2,1)S(1)}, bf16[256,2048]{0,1:T(8,128)(2,1)}, u32[]{:S(2)}) copy-start(bf16[256,2048]{0,1:T(8,128)(2,1)} %copy.120) | copy-start | bytes 3145732
  98.2 28.6 %all-to-all-start.2 = ((bf16[4,64,2048]{2,1,0:T(8,128)(2,1)}), bf16[4,64,2048]{2,1,0:T(8,128)(2,1)S(1)}, u32[]{:S(2)}, u32[]{:S(2)}) async-start(bf16[4,64,2048]{2,1,0:T(8,128)(2,1)} %bitcast.18), calls=%async_computation.2 | async-start | bytes 2097152 | tf_op jit(solution)/shard_map/all_to_all | solution.py:142
  127.8 6.2 %copy-start.1 = (f32[16,256,128]{1,2,0:T(8,128)S(1)}, f32[16,256,128]{1,2,0:T(8,128)}, u32[]{:S(2)}) copy-start(f32[16,256,128]{1,2,0:T(8,128)} %fusion.33) | copy-start | bytes 6291460
  132.0 3.6 %copy-start.9 = (f32[2048]{0:T(1024)S(1)}, f32[2048]{0:T(1024)}, u32[]{:S(2)}) copy-start(f32[2048]{0:T(1024)} %param.13) | copy-start | bytes 24580
Sparse Core Ops, SparseCore 0:
  23.6 26.9 all-gather.4
  52.5 36.7 all-gather.6
where the time goes:
time: 145 us; the launch traced here: 144 us
  matrix products  28.9 us (20%)
  blocking collectives  28.3 us (20%)
  local copies, waits for them, and re-layouts  24.9 us (17%)
  waiting for transfers between devices  24.8 us (17%)
  between operations  15 us (10%)
  other arithmetic  14.6 us (10%)
  starting transfers between devices  7.11 us (5%)
    all_to_all x1, waiting for transfers between devices, softmax_part(): lax.all_to_all(soft_q, 'head', split_axis=1, concat_axis=0, tiled=True)  19 us
    all_to_all x1, blocking collectives, softmax_part(): lax.all_to_all(soft_kv, 'head', split_axis=1, concat_axis=0, tiled=True)  15.1 us
    dot_general x8, matrix products, update(): jnp.einsum('ngqk,knd->ngqd', weights.astype(jnp.bfloat16), value_rows, pr...  13.6 us
    unnamed x1, blocking collectives  13.2 us
    reduce_sum x8, other arithmetic, update(): total = total * decay_factor + jnp.sum(weights, axis=-1)  8.02 us
    dot_general x8, matrix products, update(): jnp.einsum('qngd,knd->ngqk', queries, key_matrix, preferred_element_type=...  6.66 us
    all_to_all x1, waiting for transfers between devices, softmax_part(): lax.all_to_all(result, 'head', split_axis=0, concat_axis=1, tiled=True)  5.71 us
    dynamic_slice x8, local copies, waits for them, and re-layouts, step(): kblock = lax.dynamic_slice_in_dim(piece, index * width, width, 0)  5.34 us
  transfers between devices with their start and end apart: 4, of which 2 were waited for; matrix products, arithmetic and copies ran while one was open for 37% of the time, Pallas kernels for 0%

commit v1 on v0

--- a/solution.py
+++ b/solution.py
@@ -1,13 +1,24 @@
+import functools
 import math
 
 import jax
 import jax.numpy as jnp
 from jax import lax
+from jax.experimental import pallas as pl
+from jax.experimental.pallas import tpu as pltpu
 from jax.sharding import PartitionSpec as P
 
+MESH = pl.DeviceIdType.MESH
+
+
+def running_sum(x):
+    size = x.shape[1]
+    upper = jnp.triu(jnp.ones((size, size), x.dtype))
+    return jnp.dot(x, upper, precision=lax.Precision.HIGHEST)
+
 
 def block_local(kb, gb):
-    cum = jnp.cumsum(gb, axis=1)
+    cum = running_sum(gb)
     keys_scaled = (kb.astype(jnp.float32) * jnp.exp(cum[:, -1:] - cum).T[:, :, None]).astype(
         jnp.bfloat16
     )
@@ -46,7 +57,7 @@
     total = join_states(total, (cum[:, -1], local))
     logs = lax.all_gather(total[0][None], "ctx", axis=0, tiled=True)
     mine = lax.axis_index("ctx")
-    csum = jnp.cumsum(logs, axis=0)
+    csum = running_sum(logs.T).T
     before = jnp.sum(jnp.where((jnp.arange(logs.shape[0]) < mine)[:, None], logs, 0.0), axis=0)
     piece = lax.all_gather(total[1][None].astype(jnp.bfloat16), "ctx", axis=0, tiled=True).astype(
         jnp.float32
@@ -142,9 +153,287 @@
     return lax.all_to_all(result, "head", split_axis=0, concat_axis=1, tiled=True)
 
 
-def body(lin_q, lin_k, lin_v, log_decay, lin_gain, soft_q, soft_kv):
+def mixer_kernel(
+    nctx, nz, dim,
+    lq, lk, lv, ld, gain, sq, skv,
+    lin_out, soft_out,
+    kv_all, q_all, st_send, st_recv, tot_send, tot_recv, pre_send, state_in, cum, mix, out_send,
+    own_sem, kv_ss, kv_rs, q_ss, q_rs, z_ss, z_rs, st_ss, st_rs, tt_ss, tt_rs, pr_ss, pr_rs,
+    o_ss, o_rs,
+):
+    me = lax.axis_index("ctx")
+    zme = lax.axis_index("head")
+    tok = lq.shape[0]
+    heads = ld.shape[0]
+    rows = sq.shape[0]
+    qw = sq.shape[1] // nctx
+    group = qw // dim
+    hpo = heads // nctx
+    f32, bf16 = jnp.float32, jnp.bfloat16
+
+    def ctx_peer(k):
+        return lax.rem(me + k, nctx)
+
+    def z_peer(k):
+        return lax.rem(zme + k, nz)
+
+    barrier = pltpu.get_barrier_semaphore()
+    for k in range(1, nctx):
+        pl.semaphore_signal(barrier, inc=1, device_id=(ctx_peer(k), zme), device_id_type=MESH)
+    for k in range(1, nz):
+        pl.semaphore_signal(barrier, inc=1, device_id=(me, z_peer(k)), device_id_type=MESH)
+    pl.semaphore_wait(barrier, nctx + nz - 2)
+
+    def remote(src, dst, ss, rs, k, device):
+        return pltpu.make_async_remote_copy(
+            src_ref=src, dst_ref=dst, send_sem=ss.at[k], recv_sem=rs.at[k],
+            device_id=device, device_id_type=MESH,
+        )
+
+    def cols(index, width):
+        return pl.ds(pl.multiple_of(index * width, width), width)
+
+    def kv_copy(k):
+        d = ctx_peer(k)
+        return remote(skv.at[:, cols(d, 2 * dim)], kv_all.at[zme, me], kv_ss, kv_rs, k, (d, zme))
+
+    def q_copy(k):
+        d = ctx_peer(k)
+        return remote(sq.at[:, cols(d, qw)], q_all.at[me], q_ss, q_rs, k, (d, zme))
+
+    def z_copy(k):
+        return remote(kv_all.at[zme], kv_all.at[zme], z_ss, z_rs, k, (me, z_peer(k)))
+
+    def st_copy(k):
+        d = ctx_peer(k)
+        return remote(st_send.at[d], st_recv.at[me], st_ss, st_rs, k, (d, zme))
+
+    def tt_copy(k):
+        d = ctx_peer(k)
+        return remote(tot_send.at[d], tot_recv.at[me], tt_ss, tt_rs, k, (d, zme))
+
+    def pre_copy(k):
+        d = ctx_peer(k)
+        return remote(pre_send.at[d], state_in.at[me], pr_ss, pr_rs, k, (d, zme))
+
+    def out_copy(d, k):
+        return remote(out_send.at[d], soft_out.at[:, cols(me, qw)], o_ss, o_rs, k, (d, zme))
+
+    own_kv = pltpu.make_async_copy(skv.at[:, cols(me, 2 * dim)], kv_all.at[zme, me], own_sem.at[0])
+    own_q = pltpu.make_async_copy(sq.at[:, cols(me, qw)], q_all.at[me], own_sem.at[1])
+    own_out = pltpu.make_async_copy(
+        out_send.at[me], soft_out.at[:, cols(me, qw)], own_sem.at[2]
+    )
+    own_kv.start()
+    for k in range(1, nctx):
+        kv_copy(k).start()
+    own_q.start()
+    for k in range(1, nctx):
+        q_copy(k).start()
+
+    low = lax.broadcasted_iota(jnp.int32, (tok, tok), 1) <= lax.broadcasted_iota(
+        jnp.int32, (tok, tok), 0
+    )
+    tri = jnp.where(low, 1.0, 0.0).astype(bf16)
+
+    def running(part, wide):
+        return lax.dot_general(tri, part, (((1,), (1,)), ((), ())), preferred_element_type=f32)
+
+    def local_state(j, carry):
+        for r in range(hpo):
+            h = j * hpo + r
+            g = jnp.broadcast_to(ld[pl.ds(h, 1), :], (dim, tok))
+            g0 = g.astype(bf16)
+            rest = g - g0.astype(f32)
+            g1 = rest.astype(bf16)
+            g2 = (rest - g1.astype(f32)).astype(bf16)
+            c = running(g0, dim) + running(g1, dim) + running(g2, dim)
+            cum[h] = c
+            last = c[tok - 1 : tok, :]
+            tot_send[j, pl.ds(r, 1), :] = last
+            ks = (lk[:, cols(h, dim)].astype(f32) * jnp.exp(last - c)).astype(bf16)
+            st_send[j, r] = lax.dot_general(
+                ks, lv[:, cols(h, dim)], (((0,), (0,)), ((), ())), preferred_element_type=f32
+            ).astype(bf16)
+        return carry
+
+    tot_send[...] = jnp.zeros_like(tot_send)
+    lax.fori_loop(0, nctx, local_state, 0)
+
+    own_kv.wait()
+    for k in range(1, nctx):
+        kv_copy(k).wait_recv()
+    for k in range(1, nz):
+        z_copy(k).start()
+    for k in range(1, nctx):
+        st_copy(k).start()
+        tt_copy(k).start()
+    st_recv[me] = st_send[me]
+    tot_recv[me] = tot_send[me]
+
+    def intra(h, carry):
+        c = cum[h]
+        wide = jnp.concatenate([c] * (tok // dim), axis=1)
+        row = jnp.transpose(c)[0:1, :]
+        weight = jnp.where(low, jnp.exp(jnp.minimum(wide - row, 0.0)), 0.0)
+        s = lax.dot_general(
+            lq[:, cols(h, dim)], lk[:, cols(h, dim)], (((1,), (1,)), ((), ())),
+            preferred_element_type=f32,
+        )
+        probs = (s * weight).astype(bf16)
+        mix[h] = jnp.dot(probs, lv[:, cols(h, dim)], preferred_element_type=f32)
+        return carry
+
+    lax.fori_loop(0, heads, intra, 0)
+
+    for k in range(1, nctx):
+        st_copy(k).wait_recv()
+        tt_copy(k).wait_recv()
+    state = [jnp.zeros((dim, dim), f32) for _ in range(hpo)]
+    for c in range(nctx):
+        for r in range(hpo):
+            pre_send[c, r] = state[r].astype(bf16)
+            decay = jnp.exp(tot_recv[c, r : r + 1, :])
+            state[r] = decay * state[r] + st_recv[c, r].astype(f32)
+    for k in range(1, nctx):
+        pre_copy(k).start()
+    state_in[me] = pre_send[me]
+
+    own_q.wait()
+    for k in range(1, nctx):
+        q_copy(k).wait_recv()
+    for k in range(1, nz):
+        z_copy(k).wait_recv()
+    factor = dim ** (-0.5) * math.log2(math.e)
+    per = max(1, min(group, tok // rows))
+    for c in range(nctx):
+        for t in range(group // per):
+            q = jnp.concatenate(
+                [
+                    q_all[c, :, (t * per + i) * dim : (t * per + i + 1) * dim]
+                    for i in range(per)
+                ],
+                axis=0,
+            )
+            kd = kv_all[:, c, :, :dim].reshape(nz * rows, dim)
+            vd = kv_all[:, c, :, dim:].reshape(nz * rows, dim)
+            sd = lax.dot_general(q, kd, (((1,), (1,)), ((), ())), preferred_element_type=f32)
+            kpos = lax.broadcasted_iota(jnp.int32, sd.shape, 1)
+            qpos = zme * rows + lax.rem(lax.broadcasted_iota(jnp.int32, sd.shape, 0), rows)
+            sd = jnp.where(kpos <= qpos, sd, -1e30)
+            peak = jnp.max(sd, axis=1, keepdims=True)
+            if c > 0:
+                kp = kv_all[:, :c, :, :dim].reshape(nz * c * rows, dim)
+                vp = kv_all[:, :c, :, dim:].reshape(nz * c * rows, dim)
+                sp = lax.dot_general(q, kp, (((1,), (1,)), ((), ())), preferred_element_type=f32)
+                peak = jnp.maximum(peak, jnp.max(sp, axis=1, keepdims=True))
+            wd = jnp.exp2((sd - peak) * factor)
+            total = jnp.sum(wd, axis=1, keepdims=True)
+            acc = jnp.dot(wd.astype(bf16), vd, preferred_element_type=f32)
+            if c > 0:
+                wp = jnp.exp2((sp - peak) * factor)
+                total = total + jnp.sum(wp, axis=1, keepdims=True)
+                acc = acc + jnp.dot(wp.astype(bf16), vp, preferred_element_type=f32)
+            out = (acc / total).astype(bf16)
+            for i in range(per):
+                out_send[c, :, (t * per + i) * dim : (t * per + i + 1) * dim] = out[
+                    i * rows : (i + 1) * rows
+                ]
+
+        @pl.when(me == c)
+        def _():
+            own_out.start()
+
+        @pl.when(me != c)
+        def _():
+            out_copy(c, lax.rem(c - me + nctx, nctx)).start()
+
+    for k in range(1, nctx):
+        pre_copy(k).wait_recv()
+
+    def finish(j, carry):
+        for r in range(hpo):
+            h = j * hpo + r
+            inter = jnp.dot(lq[:, cols(h, dim)], state_in[j, r], preferred_element_type=f32)
+            m = mix[h] + jnp.exp(cum[h]) * inter
+            ms = jnp.mean(m * m, axis=1, keepdims=True)
+            lin_out[:, cols(h, dim)] = (
+                m * lax.rsqrt(ms + 1e-05) * gain[:, cols(h, dim)]
+            ).astype(bf16)
+        return carry
+
+    lax.fori_loop(0, nctx, finish, 0)
+
+    own_out.wait()
+    for k in range(1, nctx):
+        out_copy(ctx_peer(k), k).wait()
+        kv_copy(k).wait_send()
+        q_copy(k).wait_send()
+        st_copy(k).wait_send()
+        tt_copy(k).wait_send()
+        pre_copy(k).wait_send()
+    for k in range(1, nz):
+        z_copy(k).wait_send()
+
+
+def fused_body(nctx, nz, lin_q, lin_k, lin_v, log_decay, lin_gain, soft_q, soft_kv):
+    tok, width = lin_q.shape
+    heads = log_decay.shape[0]
+    dim = width // heads
+    rows = soft_q.shape[0]
+    qw = soft_q.shape[1] // nctx
+    hpo = heads // nctx
+    f32, bf16 = jnp.float32, jnp.bfloat16
+    vmem = pl.BlockSpec(memory_space=pltpu.VMEM)
+    hbm = pl.BlockSpec(memory_space=pl.ANY)
+    dma = pltpu.SemaphoreType.DMA
+    return pl.pallas_call(
+        functools.partial(mixer_kernel, nctx, nz, dim),
+        out_shape=(
+            jax.ShapeDtypeStruct(lin_q.shape, bf16),
+            jax.ShapeDtypeStruct(soft_q.shape, bf16),
+        ),
+        in_specs=[vmem] * 5 + [hbm] * 2,
+        out_specs=(vmem, hbm),
+        scratch_shapes=[
+            pltpu.VMEM((nz, nctx, rows, 2 * dim), bf16),
+            pltpu.VMEM((nctx, rows, qw), bf16),
+            pltpu.VMEM((nctx, hpo, dim, dim), bf16),
+            pltpu.VMEM((nctx, hpo, dim, dim), bf16),
+            pltpu.VMEM((nctx, 8, dim), f32),
+            pltpu.VMEM((nctx, 8, dim), f32),
+            pltpu.VMEM((nctx, hpo, dim, dim), bf16),
+            pltpu.VMEM((nctx, hpo, dim, dim), bf16),
+            pltpu.VMEM((heads, tok, dim), f32),
+            pltpu.VMEM((heads, tok, dim), f32),
+            pltpu.VMEM((nctx, rows, qw), bf16),
+            dma((3,)),
+            dma((nctx,)), dma((nctx,)),
+            dma((nctx,)), dma((nctx,)),
+            dma((nz,)), dma((nz,)),
+            dma((nctx,)), dma((nctx,)),
+            dma((nctx,)), dma((nctx,)),
+            dma((nctx,)), dma((nctx,)),
+            dma((nctx,)), dma((nctx,)),
+        ],
+        compiler_params=pltpu.CompilerParams(
+            collective_id=0, has_side_effects=True, vmem_limit_bytes=50 * 1024 * 1024
+        ),
+        cost_estimate=pl.CostEstimate(
+            flops=4 * 10**9, bytes_accessed=8 * 10**6, transcendentals=6 * 10**6
+        ),
+        name="mixers",
+    )(lin_q, lin_k, lin_v, log_decay, lin_gain.reshape(1, width), soft_q, soft_kv)
+
+
+def body(nctx, nz, lin_q, lin_k, lin_v, log_decay, lin_gain, soft_q, soft_kv):
     heads = log_decay.shape[0]
     dim = lin_q.shape[1] // heads
+    kv_heads = soft_kv.shape[1] // (2 * dim)
+    if kv_heads == nctx and heads % nctx == 0 and heads // nctx <= 8:
+        return fused_body(
+            nctx, nz, lin_q, lin_k, lin_v, log_decay, lin_gain, soft_q, soft_kv
+        )
     lin_out = lightning_part(lin_q, lin_k, lin_v, log_decay, lin_gain)
     soft_out = softmax_part(soft_q, soft_kv, dim)
     return (lin_out, soft_out)
@@ -152,7 +441,7 @@
 
 def solution(mesh):
     return jax.shard_map(
-        body,
+        functools.partial(body, mesh.shape["ctx"], mesh.shape["head"]),
         mesh=mesh,
         in_specs=(
             P("ctx", "head"),

time: 145 us -> 64.1 us (0.44)
  the two profiles are of different devices: /device:TPU:0 before, /device:TPU:15 now
where the time goes in v1:
time: 64.1 us; the launch traced here: 63.8 us
  Pallas kernels  57.6 us (90%)
  local copies, waits for them, and re-layouts  5.52 us (9%)
  between operations  0.65 us (1%)
    pallas_call x1, Pallas kernels, fused_body(): pl.pallas_call(functools.partial(mixer_kernel, nctx, nz, dim), out_shape=...  57.6 us
    unnamed x10, local copies, waits for them, and re-layouts  5.52 us

profile of v1, /device:TPU:15, one launch (start us, length us, event | category | flops | bytes accessed | tf_op | source)
XLA Modules:
  0.0 63.8 jit_solution(7615727688085230831)
XLA Ops:
  0.6 0.0 copy-start
  0.6 1.2 %copy-done = bf16[256,2048]{1,0:T(8,128)(2,1)S(1)} copy-done((bf16[256,2048]{1,0:T(8,128)(2,1)S(1)}, bf16[256,2048]{1,0:T(8,128)(2,1)}, u32[]{:S(2)}) %copy-start) | copy-done | bytes 1048600
  1.9 0.0 copy-start.1
  1.9 0.9 %copy-done.1 = bf16[64,2048]{1,0:T(8,128)(2,1)S(1)} copy-done((bf16[64,2048]{1,0:T(8,128)(2,1)S(1)}, bf16[64,2048]{1,0:T(8,128)(2,1)}, u32[]{:S(2)}) %copy-start.1) | copy-done | bytes 262168
  2.8 0.0 copy-start.2
  2.8 0.7 %copy-done.2 = f32[16,256]{1,0:T(8,128)S(1)} copy-done((f32[16,256]{1,0:T(8,128)S(1)}, f32[16,256]{1,0:T(8,128)}, u32[]{:S(2)}) %copy-start.2) | copy-done | bytes 16408
  3.5 0.0 copy-start.3
  3.5 0.7 %copy-done.3 = f32[2048]{0:T(1024)S(1)} copy-done((f32[2048]{0:T(1024)S(1)}, f32[2048]{0:T(1024)}, u32[]{:S(2)}) %copy-start.3) | copy-done | bytes 8216
  4.2 57.6 %mixers.1 = (bf16[256,2048]{1,0:T(8,128)(2,1)S(1)}, bf16[64,8192]{1,0:T(8,128)(2,1)S(1)}) custom-call(bf16[256,2048]{1,0:T(8,128)(2,1)S(1)} %copy-done, bf16[256,2048]{1,0:T(8,128)(2,1)} %lk.1, bf16[256,2048]{1,0:T(8,128)(2,1)} %lv.1, f32[16,256]{1,0:T(8,128)S(1)} %copy-done.2, f32[1,2048]{1,0:T(1,128)S(1)} %bitcast.1, bf16[64,8192]{1,0:T(8,128)(2,1)} %sq.1, ...), custom_call_target="tpu_custom_call" | custom-call | flops 4000000000 | bytes 8000000 | tf_op jit(solution)/shard_map/mixers/pallas_call | solution.py:390
  61.9 1.0 %copy.11 = bf16[256,2048]{1,0:T(8,128)(2,1)} copy(bf16[256,2048]{1,0:T(8,128)(2,1)S(1)} %get-tuple-element.4) | data formatting | bytes 2097152
  62.9 1.0 %copy.12 = bf16[64,8192]{1,0:T(8,128)(2,1)} copy(bf16[64,8192]{1,0:T(8,128)(2,1)S(1)} %get-tuple-element.5) | data formatting | bytes 2097152
Async XLA Ops:
  0.6 1.2 %copy-start = (bf16[256,2048]{1,0:T(8,128)(2,1)S(1)}, bf16[256,2048]{1,0:T(8,128)(2,1)}, u32[]{:S(2)}) copy-start(bf16[256,2048]{1,0:T(8,128)(2,1)} %lq.1) | copy-start | bytes 3145732
  1.9 0.9 %copy-start.1 = (bf16[64,2048]{1,0:T(8,128)(2,1)S(1)}, bf16[64,2048]{1,0:T(8,128)(2,1)}, u32[]{:S(2)}) copy-start(bf16[64,2048]{1,0:T(8,128)(2,1)} %skv.1) | copy-start | bytes 786436
  2.8 0.7 %copy-start.2 = (f32[16,256]{1,0:T(8,128)S(1)}, f32[16,256]{1,0:T(8,128)}, u32[]{:S(2)}) copy-start(f32[16,256]{1,0:T(8,128)} %ld.1) | copy-start | bytes 49156
  3.5 0.7 %copy-start.3 = (f32[2048]{0:T(1024)S(1)}, f32[2048]{0:T(1024)}, u32[]{:S(2)}) copy-start(f32[2048]{0:T(1024)} %param.11) | copy-start | bytes 24580

commit v2 on v1

--- a/solution.py
+++ b/solution.py
@@ -155,10 +155,10 @@
 
 def mixer_kernel(
     nctx, nz, dim,
-    lq, lk, lv, ld, gain, sq, skv,
+    lq_in, lk_in, lv_in, ld_in, gain_in, sq, skv,
     lin_out, soft_out,
     kv_all, q_all, st_send, st_recv, tot_send, tot_recv, pre_send, state_in, cum, mix, out_send,
-    own_sem, kv_ss, kv_rs, q_ss, q_rs, z_ss, z_rs, st_ss, st_rs, tt_ss, tt_rs, pr_ss, pr_rs,
+    lq, lk, lv, ld, gain, in_sem, own_sem, kv_ss, kv_rs, q_ss, q_rs, z_ss, z_rs, st_ss, st_rs, tt_ss, tt_rs, pr_ss, pr_rs,
     o_ss, o_rs,
 ):
     me = lax.axis_index("ctx")
@@ -177,11 +177,19 @@
     def z_peer(k):
         return lax.rem(zme + k, nz)
 
+    loads = [
+        pltpu.make_async_copy(src, dst, in_sem.at[i])
+        for i, (src, dst) in enumerate(
+            [(ld_in, ld), (lk_in, lk), (lv_in, lv), (lq_in, lq), (gain_in, gain)]
+        )
+    ]
     barrier = pltpu.get_barrier_semaphore()
     for k in range(1, nctx):
         pl.semaphore_signal(barrier, inc=1, device_id=(ctx_peer(k), zme), device_id_type=MESH)
     for k in range(1, nz):
         pl.semaphore_signal(barrier, inc=1, device_id=(me, z_peer(k)), device_id_type=MESH)
+    for load in loads:
+        load.start()
     pl.semaphore_wait(barrier, nctx + nz - 2)
 
     def remote(src, dst, ss, rs, k, device):
@@ -201,8 +209,32 @@
         d = ctx_peer(k)
         return remote(sq.at[:, cols(d, qw)], q_all.at[me], q_ss, q_rs, k, (d, zme))
 
-    def z_copy(k):
-        return remote(kv_all.at[zme], kv_all.at[zme], z_ss, z_rs, k, (me, z_peer(k)))
+    def z_copy(src, step):
+        to = jnp.clip(zme + step, 0, nz - 1)
+        slot = src if step > 0 else nz + src
+        return pltpu.make_async_remote_copy(
+            src_ref=kv_all.at[src], dst_ref=kv_all.at[src], send_sem=z_ss.at[slot],
+            recv_sem=z_rs.at[src], device_id=(me, to), device_id_type=MESH,
+        )
+
+    def z_relay(away):
+        @pl.when(zme >= away)
+        def _():
+            if away > 0:
+                z_copy(zme - away, 1).wait_recv()
+
+            @pl.when(zme < nz - 1)
+            def _():
+                z_copy(zme - away, 1).start()
+
+        @pl.when(zme < nz - away)
+        def _():
+            if away > 0:
+                z_copy(zme + away, -1).wait_recv()
+
+            @pl.when(zme > 0)
+            def _():
+                z_copy(zme + away, -1).start()
 
     def st_copy(k):
         d = ctx_peer(k)
@@ -258,13 +290,14 @@
         return carry
 
     tot_send[...] = jnp.zeros_like(tot_send)
+    for load in loads:
+        load.wait()
     lax.fori_loop(0, nctx, local_state, 0)
 
     own_kv.wait()
     for k in range(1, nctx):
         kv_copy(k).wait_recv()
-    for k in range(1, nz):
-        z_copy(k).start()
+    z_relay(0)
     for k in range(1, nctx):
         st_copy(k).start()
         tt_copy(k).start()
@@ -284,7 +317,10 @@
         mix[h] = jnp.dot(probs, lv[:, cols(h, dim)], preferred_element_type=f32)
         return carry
 
-    lax.fori_loop(0, heads, intra, 0)
+    for part in range(1, nz):
+        lax.fori_loop(heads * (part - 1) // (nz - 1), heads * part // (nz - 1), intra, 0)
+        if part < nz - 1:
+            z_relay(part)
 
     for k in range(1, nctx):
         st_copy(k).wait_recv()
@@ -302,11 +338,10 @@
     own_q.wait()
     for k in range(1, nctx):
         q_copy(k).wait_recv()
-    for k in range(1, nz):
-        z_copy(k).wait_recv()
+    z_relay(nz - 1)
     factor = dim ** (-0.5) * math.log2(math.e)
     per = max(1, min(group, tok // rows))
-    for c in range(nctx):
+    def attend(c):
         for t in range(group // per):
             q = jnp.concatenate(
                 [
@@ -340,13 +375,21 @@
                     i * rows : (i + 1) * rows
                 ]
 
-        @pl.when(me == c)
+    def turn(k, carry):
+        c = ctx_peer(k)
+        lax.switch(c, [functools.partial(attend, i) for i in range(nctx)])
+
+        @pl.when(k == nctx)
         def _():
             own_out.start()
 
-        @pl.when(me != c)
+        @pl.when(k < nctx)
         def _():
-            out_copy(c, lax.rem(c - me + nctx, nctx)).start()
+            out_copy(c, k).start()
+
+        return carry
+
+    lax.fori_loop(1, nctx + 1, turn, 0)
 
     for k in range(1, nctx):
         pre_copy(k).wait_recv()
@@ -372,8 +415,15 @@
         st_copy(k).wait_send()
         tt_copy(k).wait_send()
         pre_copy(k).wait_send()
-    for k in range(1, nz):
-        z_copy(k).wait_send()
+    for away in range(nz):
+
+        @pl.when((zme >= away) & (zme < nz - 1))
+        def _(away=away):
+            z_copy(zme - away, 1).wait_send()
+
+        @pl.when((zme < nz - away) & (zme > 0))
+        def _(away=away):
+            z_copy(zme + away, -1).wait_send()
 
 
 def fused_body(nctx, nz, lin_q, lin_k, lin_v, log_decay, lin_gain, soft_q, soft_kv):
@@ -385,7 +435,8 @@
     hpo = heads // nctx
     f32, bf16 = jnp.float32, jnp.bfloat16
     vmem = pl.BlockSpec(memory_space=pltpu.VMEM)
-    hbm = pl.BlockSpec(memory_space=pl.ANY)
+    hbm = pl.BlockSpec(memory_space=pltpu.HBM)
+    anywhere = pl.BlockSpec(memory_space=pl.ANY)
     dma = pltpu.SemaphoreType.DMA
     return pl.pallas_call(
         functools.partial(mixer_kernel, nctx, nz, dim),
@@ -393,8 +444,8 @@
             jax.ShapeDtypeStruct(lin_q.shape, bf16),
             jax.ShapeDtypeStruct(soft_q.shape, bf16),
         ),
-        in_specs=[vmem] * 5 + [hbm] * 2,
-        out_specs=(vmem, hbm),
+        in_specs=[hbm] * 7,
+        out_specs=(vmem, anywhere),
         scratch_shapes=[
             pltpu.VMEM((nz, nctx, rows, 2 * dim), bf16),
             pltpu.VMEM((nctx, rows, qw), bf16),
@@ -407,10 +458,16 @@
             pltpu.VMEM((heads, tok, dim), f32),
             pltpu.VMEM((heads, tok, dim), f32),
             pltpu.VMEM((nctx, rows, qw), bf16),
+            pltpu.VMEM(lin_q.shape, bf16),
+            pltpu.VMEM(lin_q.shape, bf16),
+            pltpu.VMEM(lin_q.shape, bf16),
+            pltpu.VMEM(log_decay.shape, f32),
+            pltpu.VMEM((1, width), f32),
+            dma((5,)),
             dma((3,)),
             dma((nctx,)), dma((nctx,)),
             dma((nctx,)), dma((nctx,)),
-            dma((nz,)), dma((nz,)),
+            dma((2 * nz,)), dma((nz,)),
             dma((nctx,)), dma((nctx,)),
             dma((nctx,)), dma((nctx,)),
             dma((nctx,)), dma((nctx,)),

time: 64.1 us -> 56.6 us (0.88)
  the two profiles are of different devices: /device:TPU:15 before, /device:TPU:7 now
where the time goes in v2:
time: 56.6 us; the launch traced here: 56.3 us
  Pallas kernels  50.1 us (89%)
  local copies, waits for them, and re-layouts  5.52 us (10%)
  between operations  0.65 us (1%)
    pallas_call x1, Pallas kernels, fused_body(): pl.pallas_call(functools.partial(mixer_kernel, nctx, nz, dim), out_shape=...  50.1 us
    unnamed x10, local copies, waits for them, and re-layouts  5.52 us

profile of v2, /device:TPU:7, one launch (start us, length us, event | category | flops | bytes accessed | tf_op | source)
XLA Modules:
  0.0 56.3 jit_solution(1016578541011674166)
XLA Ops:
  0.6 0.0 copy-start
  0.6 1.2 %copy-done = bf16[256,2048]{1,0:T(8,128)(2,1)S(1)} copy-done((bf16[256,2048]{1,0:T(8,128)(2,1)S(1)}, bf16[256,2048]{1,0:T(8,128)(2,1)}, u32[]{:S(2)}) %copy-start) | copy-done | bytes 1048600
  1.9 0.0 copy-start.1
  1.9 0.9 %copy-done.1 = bf16[64,2048]{1,0:T(8,128)(2,1)S(1)} copy-done((bf16[64,2048]{1,0:T(8,128)(2,1)S(1)}, bf16[64,2048]{1,0:T(8,128)(2,1)}, u32[]{:S(2)}) %copy-start.1) | copy-done | bytes 262168
  2.8 0.0 copy-start.2
  2.8 0.7 %copy-done.2 = f32[16,256]{1,0:T(8,128)S(1)} copy-done((f32[16,256]{1,0:T(8,128)S(1)}, f32[16,256]{1,0:T(8,128)}, u32[]{:S(2)}) %copy-start.2) | copy-done | bytes 16408
  3.5 0.0 copy-start.3
  3.5 0.7 %copy-done.3 = f32[2048]{0:T(1024)S(1)} copy-done((f32[2048]{0:T(1024)S(1)}, f32[2048]{0:T(1024)}, u32[]{:S(2)}) %copy-start.3) | copy-done | bytes 8216
  4.2 50.1 %mixers.1 = (bf16[256,2048]{1,0:T(8,128)(2,1)S(1)}, bf16[64,8192]{1,0:T(8,128)(2,1)S(1)}) custom-call(bf16[256,2048]{1,0:T(8,128)(2,1)S(1)} %copy-done, bf16[256,2048]{1,0:T(8,128)(2,1)} %lk_in.1, bf16[256,2048]{1,0:T(8,128)(2,1)} %lv_in.1, f32[16,256]{1,0:T(8,128)S(1)} %copy-done.2, f32[1,2048]{1,0:T(1,128)S(1)} %bitcast.1, bf16[64,8192]{1,0:T(8,128)(2,1)} %sq.1, ...), custom_call_target="tpu_custom_call" | custom-call | flops 4000000000 | bytes 8000000 | tf_op jit(solution)/shard_map/mixers/pallas_call | solution.py:441
  54.4 1.0 %copy.11 = bf16[256,2048]{1,0:T(8,128)(2,1)} copy(bf16[256,2048]{1,0:T(8,128)(2,1)S(1)} %get-tuple-element.4) | data formatting | bytes 2097152
  55.3 1.0 %copy.12 = bf16[64,8192]{1,0:T(8,128)(2,1)} copy(bf16[64,8192]{1,0:T(8,128)(2,1)S(1)} %get-tuple-element.5) | data formatting | bytes 2097152
Async XLA Ops:
  0.6 1.2 %copy-start = (bf16[256,2048]{1,0:T(8,128)(2,1)S(1)}, bf16[256,2048]{1,0:T(8,128)(2,1)}, u32[]{:S(2)}) copy-start(bf16[256,2048]{1,0:T(8,128)(2,1)} %lq_in.1) | copy-start | bytes 3145732
  1.9 0.9 %copy-start.1 = (bf16[64,2048]{1,0:T(8,128)(2,1)S(1)}, bf16[64,2048]{1,0:T(8,128)(2,1)}, u32[]{:S(2)}) copy-start(bf16[64,2048]{1,0:T(8,128)(2,1)} %skv.1) | copy-start | bytes 786436
  2.8 0.7 %copy-start.2 = (f32[16,256]{1,0:T(8,128)S(1)}, f32[16,256]{1,0:T(8,128)}, u32[]{:S(2)}) copy-start(f32[16,256]{1,0:T(8,128)} %ld_in.1) | copy-start | bytes 49156
  3.5 0.7 %copy-start.3 = (f32[2048]{0:T(1024)S(1)}, f32[2048]{0:T(1024)}, u32[]{:S(2)}) copy-start(f32[2048]{0:T(1024)} %param.11) | copy-start | bytes 24580

commit v3 on v2

--- a/solution.py
+++ b/solution.py
@@ -259,9 +259,6 @@
     own_kv.start()
     for k in range(1, nctx):
         kv_copy(k).start()
-    own_q.start()
-    for k in range(1, nctx):
-        q_copy(k).start()
 
     low = lax.broadcasted_iota(jnp.int32, (tok, tok), 1) <= lax.broadcasted_iota(
         jnp.int32, (tok, tok), 0
@@ -301,6 +298,9 @@
     for k in range(1, nctx):
         st_copy(k).start()
         tt_copy(k).start()
+    own_q.start()
+    for k in range(1, nctx):
+        q_copy(k).start()
     st_recv[me] = st_send[me]
     tot_recv[me] = tot_send[me]
 

time: 56.6 us -> 57.3 us (1.012)
  Pallas kernels: 50.1 us -> 50.8 us
    pallas_call x1, Pallas kernels: 50.1 us -> 50.8 us  [fused_body(): pl.pallas_call(functools.partial(mixer_kernel, nctx, nz, dim), out_shape=...]
where the time goes in v3:
time: 57.3 us; the launch traced here: 56.9 us
  Pallas kernels  50.8 us (89%)
  local copies, waits for them, and re-layouts  5.52 us (10%)
  between operations  0.65 us (1%)
    pallas_call x1, Pallas kernels, fused_body(): pl.pallas_call(functools.partial(mixer_kernel, nctx, nz, dim), out_shape=...  50.8 us
    unnamed x10, local copies, waits for them, and re-layouts  5.52 us

profile of v3, /device:TPU:7, one launch (start us, length us, event | category | flops | bytes accessed | tf_op | source)
XLA Modules:
  0.0 56.9 jit_solution(13244554615399011885)
XLA Ops:
  0.6 0.0 copy-start
  0.6 1.2 %copy-done = bf16[256,2048]{1,0:T(8,128)(2,1)S(1)} copy-done((bf16[256,2048]{1,0:T(8,128)(2,1)S(1)}, bf16[256,2048]{1,0:T(8,128)(2,1)}, u32[]{:S(2)}) %copy-start) | copy-done | bytes 1048600
  1.9 0.0 copy-start.1
  1.9 0.9 %copy-done.1 = bf16[64,2048]{1,0:T(8,128)(2,1)S(1)} copy-done((bf16[64,2048]{1,0:T(8,128)(2,1)S(1)}, bf16[64,2048]{1,0:T(8,128)(2,1)}, u32[]{:S(2)}) %copy-start.1) | copy-done | bytes 262168
  2.8 0.0 copy-start.2
  2.8 0.7 %copy-done.2 = f32[16,256]{1,0:T(8,128)S(1)} copy-done((f32[16,256]{1,0:T(8,128)S(1)}, f32[16,256]{1,0:T(8,128)}, u32[]{:S(2)}) %copy-start.2) | copy-done | bytes 16408
  3.5 0.0 copy-start.3
  3.5 0.7 %copy-done.3 = f32[2048]{0:T(1024)S(1)} copy-done((f32[2048]{0:T(1024)S(1)}, f32[2048]{0:T(1024)}, u32[]{:S(2)}) %copy-start.3) | copy-done | bytes 8216
  4.2 50.8 %mixers.1 = (bf16[256,2048]{1,0:T(8,128)(2,1)S(1)}, bf16[64,8192]{1,0:T(8,128)(2,1)S(1)}) custom-call(bf16[256,2048]{1,0:T(8,128)(2,1)S(1)} %copy-done, bf16[256,2048]{1,0:T(8,128)(2,1)} %lk_in.1, bf16[256,2048]{1,0:T(8,128)(2,1)} %lv_in.1, f32[16,256]{1,0:T(8,128)S(1)} %copy-done.2, f32[1,2048]{1,0:T(1,128)S(1)} %bitcast.1, bf16[64,8192]{1,0:T(8,128)(2,1)} %sq.1, ...), custom_call_target="tpu_custom_call" | custom-call | flops 4000000000 | bytes 8000000 | tf_op jit(solution)/shard_map/mixers/pallas_call | solution.py:441
  55.0 1.0 %copy.11 = bf16[256,2048]{1,0:T(8,128)(2,1)} copy(bf16[256,2048]{1,0:T(8,128)(2,1)S(1)} %get-tuple-element.4) | data formatting | bytes 2097152
  56.0 1.0 %copy.12 = bf16[64,8192]{1,0:T(8,128)(2,1)} copy(bf16[64,8192]{1,0:T(8,128)(2,1)S(1)} %get-tuple-element.5) | data formatting | bytes 2097152
Async XLA Ops:
  0.6 1.2 %copy-start = (bf16[256,2048]{1,0:T(8,128)(2,1)S(1)}, bf16[256,2048]{1,0:T(8,128)(2,1)}, u32[]{:S(2)}) copy-start(bf16[256,2048]{1,0:T(8,128)(2,1)} %lq_in.1) | copy-start | bytes 3145732
  1.9 0.9 %copy-start.1 = (bf16[64,2048]{1,0:T(8,128)(2,1)S(1)}, bf16[64,2048]{1,0:T(8,128)(2,1)}, u32[]{:S(2)}) copy-start(bf16[64,2048]{1,0:T(8,128)(2,1)} %skv.1) | copy-start | bytes 786436
  2.8 0.7 %copy-start.2 = (f32[16,256]{1,0:T(8,128)S(1)}, f32[16,256]{1,0:T(8,128)}, u32[]{:S(2)}) copy-start(f32[16,256]{1,0:T(8,128)} %ld_in.1) | copy-start | bytes 49156
  3.5 0.7 %copy-start.3 = (f32[2048]{0:T(1024)S(1)}, f32[2048]{0:T(1024)}, u32[]{:S(2)}) copy-start(f32[2048]{0:T(1024)} %param.11) | copy-start | bytes 24580
